TPU v7x, 256 devices: a whole 4x4x8 slice. The times are simulated.
256 devices in a mesh: prow: 64 (over x, z, core), pcol: 4 (over y).
Axes of the slice: x: 4, y: 4, z: 8, core: 2. Of those that a mesh axis runs over, the one named last changes fastest.
Arguments:
- matrix: float32 [24576, 15360], P('prow', 'pcol'), may hold values from -6 to 6
- lower_panel: float32 [24576, 256], P(('prow', 'pcol')), may hold values from -0.375 to 0.375
- inverse: float32 [256, 256], P('pcol'), as said below
- pivots: int32 [256], replicated, may hold values from 0 to 24575, as said below
Outputs:
- updated: float32 [24576, 15360], P('prow', 'pcol')
Inputs may be any that keep to these rules, and one draw needn't show every extreme that they name: pivots[i] is at least i; some entry equals 24575. inverse is unit lower triangular.
All inputs are finite; a program needn't handle non-finite values.
Results may differ from a plain program's by a relative error of at most 0.0003.
Values sent between devices are 32-bit elements; how exact they have to be, the bound alone decides.
A program may use at most 64 MiB of HBM per device.

v0:
```python
import jax
import jax.numpy as jnp
from jax import lax
from jax.sharding import PartitionSpec as P

BLOCK = 128


def order_lookup(pivots, queries):
    panel_width = pivots.shape[0]
    columns = jnp.arange(panel_width, dtype=jnp.int32)
    positions = jnp.concatenate([columns, pivots])
    slot_count = positions.shape[0]
    slot_ids = jnp.arange(slot_count, dtype=jnp.int32)
    same_pos = positions[:, None] == positions[None, :]
    canonical = jnp.min(jnp.where(same_pos, slot_ids[None, :], slot_count), axis=1)

    def turn(turn_index, content):
        first_slot = canonical[turn_index]
        second_slot = canonical[panel_width + turn_index]
        first_val = content[first_slot]
        second_val = content[second_slot]
        content = content.at[first_slot].set(second_val)
        return content.at[second_slot].set(first_val)

    content = lax.fori_loop(0, panel_width, turn, positions)
    matched = positions[None, :] == queries[:, None]
    first_match = jnp.min(jnp.where(matched, slot_ids[None, :], slot_count), axis=1)
    found = first_match < slot_count
    mapped = jnp.take(content, jnp.clip(first_match, 0, slot_count - 1))
    return jnp.where(found, mapped, queries)


def local(matrix, lower_panel, inverse, pivots):
    rows_dev = matrix.shape[0]
    cols_dev = matrix.shape[1]
    panel_width = inverse.shape[1]
    row_count = lax.axis_size("prow")
    my_row = lax.axis_index("prow")
    top_blocks = panel_width // BLOCK
    local_rows = jnp.arange(rows_dev, dtype=jnp.int32)
    global_rows = (local_rows // BLOCK * row_count + my_row) * BLOCK + local_rows % BLOCK
    all_queries = jnp.concatenate([global_rows, jnp.arange(panel_width, dtype=jnp.int32)])
    looked_up = order_lookup(pivots, all_queries)
    source = looked_up[:rows_dev]
    top_source = looked_up[rows_dev:]
    owner_row = top_source // BLOCK % row_count
    local_index = top_source // BLOCK // row_count * BLOCK + top_source % BLOCK
    new_part = jnp.where((owner_row == my_row)[:, None], jnp.take(matrix, local_index, axis=0), 0.0)
    block_ids = jnp.arange(top_blocks, dtype=jnp.int32)
    orig_part = jnp.where((block_ids == my_row)[:, None, None], matrix[None, :BLOCK], 0.0)
    top_orig = lax.psum(orig_part.reshape(panel_width, cols_dev), "prow")
    moved_rows = source < panel_width
    swapped = jnp.where(
        moved_rows[:, None],
        jnp.take(top_orig, jnp.clip(source, 0, panel_width - 1), axis=0),
        matrix,
    )
    strips = (
        lax.all_gather(lower_panel, "pcol", axis=0, tiled=True),
        lax.all_gather(inverse, "pcol", axis=0, tiled=True),
    )
    panel_rows = strips[0]
    full_inverse = strips[1]
    gathered = lax.psum(new_part, "prow")
    u_rows = jnp.dot(
        full_inverse, gathered, precision=lax.Precision.HIGHEST, preferred_element_type=jnp.float32
    )
    result = swapped - jnp.dot(
        panel_rows, u_rows, precision=lax.Precision.HIGHEST, preferred_element_type=jnp.float32
    )
    head_rows = lax.dynamic_slice_in_dim(
        u_rows, jnp.minimum(my_row, top_blocks - 1) * BLOCK, BLOCK, 0
    )
    first_block = jnp.where(my_row < top_blocks, head_rows, result[:BLOCK])
    return jnp.concatenate([first_block, result[BLOCK:]], axis=0)


def solution(mesh):
    return jax.shard_map(
        local,
        mesh=mesh,
        in_specs=(P("prow", "pcol"), P(("prow", "pcol"), None), P("pcol", None), P()),
        out_specs=P("prow", "pcol"),
        check_vma=False,
    )
```

profile of v0, /device:TPU:1, one launch (start us, length us, event | category | flops | bytes accessed | tf_op | source)
XLA Modules:
  0.0 1850.6 jit_solution(14528730427821727740)
XLA Ops:
  7.9 1580.9 %while.17 = (s32[]{:T(128)}, s32[512]{0:T(512)S(1)}, s32[512]{0:T(512)S(1)}, s32[]{:T(128)}, s32[]{:T(128)}, /*index=5*/s32[]{:T(128)}, s32[]{:T(128)}, s32[]{:T(128)}, s32[]{:T(128)}) while((s32[]{:T(128)}, s32[512]{0:T(512)S(1)}, s32[512]{0:T(512)S(1)}, s32[]{:T(128)}, s32[]{:T(128)}, /*index=5*/s32[]{:T(128)}, s32[]{:T(128)}, s32[]{:T(128)}, ...), condition=%wide.region_3.4_spmd, body=%wide.region_2.3_spmd.sunk | while | flops 20 | bytes 2355 | solution.py:26
  12.7 0.7 select_dynamic-update-slice_fusion.4
  13.4 0.7 select_dynamic-update-slice_fusion.5
  18.9 0.7 select_dynamic-update-slice_fusion.4
  19.6 0.7 select_dynamic-update-slice_fusion.5
  25.0 0.7 select_dynamic-update-slice_fusion.4
  37.4 0.7 select_dynamic-update-slice_fusion.4
  38.1 0.7 select_dynamic-update-slice_fusion.5
  43.6 0.7 select_dynamic-update-slice_fusion.4
  44.3 0.7 select_dynamic-update-slice_fusion.5
  49.7 0.7 select_dynamic-update-slice_fusion.4
  50.5 0.7 select_dynamic-update-slice_fusion.5
  55.9 0.7 select_dynamic-update-slice_fusion.4
  56.6 0.7 select_dynamic-update-slice_fusion.5
  62.1 0.7 select_dynamic-update-slice_fusion.4
  62.8 0.7 select_dynamic-update-slice_fusion.5
  75.2 0.7 select_dynamic-update-slice_fusion.5
  80.6 0.7 select_dynamic-update-slice_fusion.4
  81.3 0.7 select_dynamic-update-slice_fusion.5
  86.8 0.7 select_dynamic-update-slice_fusion.4
  87.5 0.7 select_dynamic-update-slice_fusion.5
  93.0 0.7 select_dynamic-update-slice_fusion.4
  93.7 0.7 select_dynamic-update-slice_fusion.5
  99.1 0.7 select_dynamic-update-slice_fusion.4
  99.9 0.7 select_dynamic-update-slice_fusion.5
  105.3 0.7 select_dynamic-update-slice_fusion.4
  112.2 0.7 select_dynamic-update-slice_fusion.5
  117.7 0.7 select_dynamic-update-slice_fusion.4
  118.4 0.7 select_dynamic-update-slice_fusion.5
  123.8 0.7 select_dynamic-update-slice_fusion.4
  124.6 0.7 select_dynamic-update-slice_fusion.5
  130.0 0.7 select_dynamic-update-slice_fusion.4
  130.7 0.7 select_dynamic-update-slice_fusion.5
  136.2 0.7 select_dynamic-update-slice_fusion.4
  136.9 0.7 select_dynamic-update-slice_fusion.5
  142.4 0.7 select_dynamic-update-slice_fusion.4
  154.7 0.7 select_dynamic-update-slice_fusion.4
  1588.8 4.3 gather_fusion
  1593.2 8.3 gather_fusion.1
  1601.6 6.6 bitcast_select_fusion
  1608.3 0.8 copy-done.2
  1609.1 11.2 all_gather.6
  1620.3 10.9 all_gather.7
  1631.3 183.3 %all-reduce.3.cloned.1.call-done = (f32[256,3840]{1,0:T(8,128)}, f32[256,3840]{1,0:T(8,128)}) async-done(((f32[256,3840]{1,0:T(8,128)}, f32[256,3840]{1,0:T(8,128)}), (f32[256,3840]{1,0:T(8,128)}, f32[256,3840]{1,0:T(8,128)})) %all-reduce.3.cloned.1.call-update) | async-done | bytes 7864336 | tf_op jit(solution)/shard_map/psum | solution.py:65
  1814.6 10.1 gather_fusion.2
  1824.6 6.2 fusion.16
  1830.9 9.4 fusion
  1840.8 3.0 pad_maximum_fusion
  (1018 shorter events, 647.9 us)
Async XLA Ops:
  6.5 1808.0 %all-reduce.3.cloned.1.call-start = ((), (), s32[]{:S(2)}) async-start(), calls=%async_computation | async-start | bytes 15728640 | tf_op jit(solution)/shard_map/psum | solution.py:65
  1593.2 8.4 slice-start
  1608.2 0.8 copy-start.2
  1608.2 12.1 copy-start.1
  1824.6 6.3 copy-start
Sparse Core Ops, SparseCore 0:
  1608.4 206.1 all-reduce.2
where the time goes:
time: 1870 us; the launch traced here: 1850 us
  loops' own time  909 us (49%)
  other arithmetic  383 us (20%)
  local copies, waits for them, and re-layouts  324 us (17%)
  waiting for transfers between devices  183 us (10%)
  blocking collectives  22.2 us (1%)
    another operation x1, loops' own time, order_lookup(): content = lax.fori_loop(0, panel_width, turn, positions)  909 us
    scatter x256, other arithmetic, turn(): content = content.at[first_slot].set(second_val)  186 us
    scatter x256, other arithmetic, turn(): return content.at[second_slot].set(first_val)  186 us
    psum x1, waiting for transfers between devices, local(): gathered = lax.psum(new_part, 'prow')  183 us
    dynamic_slice x256, local copies, waits for them, and re-layouts, turn(): second_slot = canonical[panel_width + turn_index]  152 us
    another operation x256, local copies, waits for them, and re-layouts  148 us
  transfers between devices with their start and end apart: 1, of which 1 were waited for; matrix products, arithmetic and copies ran while one was open for 0% of the time, Pallas kernels for 0%

commit v1 on v0

v1 whole, which is shorter than its diff:
```python
import functools

import jax
import jax.numpy as jnp
from jax import lax
from jax.experimental import pallas as pl
from jax.experimental.pallas import tpu as pltpu
from jax.sharding import PartitionSpec as P

BLOCK = 128
NB = 256
CAP = 16
NX, NZ, NY = 4, 8, 4
CHIPS = NX * NZ
TILES = 30
COLS = TILES * 128
ROWS = 384
MESH = pl.DeviceIdType.MESH
f32 = jnp.float32
i32 = jnp.int32
bf16 = jnp.bfloat16


def plan_kernel(p_ref, mat, tab, comp, tab_s, sem, row_sems):
    me = lax.axis_index("prow")
    core = (me % 2).astype(f32)
    mef = me.astype(f32)
    big = (NB, NB)
    I = lax.broadcasted_iota(i32, big, 0)
    J = lax.broadcasted_iota(i32, big, 1)
    Jf = J.astype(f32)
    eye = I == J
    lt = J < I
    PB = jnp.broadcast_to(p_ref[...].astype(f32), big)

    def to_col(row_b):
        return jnp.sum(jnp.where(eye, row_b, 0.0), axis=1, keepdims=True)

    def to_row(col):
        return jnp.sum(jnp.where(eye, jnp.broadcast_to(col, big), 0.0), axis=0, keepdims=True)

    def pick(col_idx, row_vals):
        return jnp.sum(jnp.where(Jf == col_idx, jnp.broadcast_to(row_vals, big), 0.0), axis=1, keepdims=True)

    p_col = to_col(PB)
    eq = (p_col == PB) & lt
    prev = jnp.max(jnp.where(eq, Jf, -1.0), axis=1, keepdims=True)
    later = jnp.max(jnp.where(eq, 1.0, 0.0), axis=0, keepdims=True)
    par = jnp.max(jnp.where((PB == I.astype(f32)) & lt, Jf, -1.0), axis=1, keepdims=True)
    icol = lax.broadcasted_iota(i32, (NB, 1), 0).astype(f32)
    root = jnp.where(par < 0.0, icol, par)

    def more(state):
        return state[1] > 0.0

    def double(state):
        r, _ = state
        nr = pick(r, to_row(r))
        return nr, jnp.max(r - nr)

    root, _ = lax.while_loop(more, double, (root, jnp.float32(1.0)))
    c_row = to_row(root)
    ts = jnp.where(prev >= 0.0, pick(prev, c_row), p_col)
    tsi = ts.astype(i32)
    owner_i = lax.shift_right_logical(tsi, 7) & 63
    owner = owner_i.astype(f32)
    lidx = (lax.shift_right_logical(tsi, 13) * BLOCK + (tsi & 127)).astype(f32)
    slot = jnp.sum(jnp.where((owner == jnp.broadcast_to(to_row(owner), big)) & lt, 1.0, 0.0), axis=1, keepdims=True)
    last_c = jnp.broadcast_to(jnp.where(later > 0.0, 0.0, c_row), big)
    w = jnp.sum(jnp.where(ts == PB, last_c, 0.0), axis=1, keepdims=True)
    out_row = ts >= float(NB)
    flag = jnp.max(slot) >= float(CAP)
    mine_core = (owner_i & 1).astype(f32) == core
    chip = lax.shift_right_logical(owner_i, 1).astype(f32)
    flat = jnp.where(mine_core, chip * CAP + slot, float(CHIPS * CAP))
    flat = jnp.minimum(flat, float(CHIPS * CAP))
    src_row = to_row(flat)
    S = lax.broadcasted_iota(i32, (NB, CHIPS * CAP), 1).astype(f32)
    ret = jnp.sum(jnp.where((flat == S) & (slot < float(CAP)) & out_row, w, 0.0), axis=0, keepdims=True)
    ret = jnp.clip(ret, 0.0, NB - 1.0)
    K = lax.broadcasted_iota(i32, (NB, 128), 1).astype(f32)
    own = (owner == mef) & (slot == K)
    gath = jnp.max(jnp.where(own, lidx, 0.0), axis=0, keepdims=True)
    dest = jnp.max(jnp.where(own & out_row, lidx, -1.0), axis=0, keepdims=True)
    tab[...] = jnp.zeros((8, 512), i32)
    tab[0:1, 0:NB] = src_row.astype(i32)
    tab[1:2, :] = ret.astype(i32)
    tab[2:3, 0:128] = gath.astype(i32)
    tab[3:4, 0:128] = dest.astype(i32)
    tab[4:5, 0:NB] = to_row(ts).astype(i32)
    tab[5:6, 0:NB] = to_row(w).astype(i32)
    tab[6:7, 0:128] = jnp.broadcast_to(jnp.where(flag, 1, 0), (1, 128)).astype(i32)
    copy = pltpu.make_async_copy(tab.at[2:3, 0:128], tab_s, sem)
    copy.start()
    copy.wait()
    copies = []
    for k in range(CAP):
        row = tab_s[0, k]
        copies.append(pltpu.make_async_copy(mat.at[pl.ds(row, 1), :], comp.at[pl.ds(k, 1), :], row_sems.at[k]))
    for copy in copies:
        copy.start()
    for copy in copies:
        copy.wait()


def plan(pivots, matrix):
    vm = pl.BlockSpec(memory_space=pltpu.VMEM)
    return pl.pallas_call(
        plan_kernel,
        out_shape=(jax.ShapeDtypeStruct((8, 512), i32), jax.ShapeDtypeStruct((CAP, COLS), f32)),
        in_specs=[vm, pl.BlockSpec(memory_space=pl.ANY)],
        out_specs=(vm, vm),
        scratch_shapes=[
            pltpu.SMEM((1, 128), i32),
            pltpu.SemaphoreType.DMA,
            pltpu.SemaphoreType.DMA((CAP,)),
        ],
        compiler_params=pltpu.CompilerParams(vmem_limit_bytes=24 << 20),
        name="plan",
    )(pivots.reshape(1, NB), matrix)


def move_kernel(tab, comp, mat, lp, inv, u, sw, lg, nr, top, psib, invf, orig, ret,
                s_nr, r_nr, s_or, r_or, s_y, r_inv, r_lp, s_sib, r_psib, r_osib, s_ret, r_ret, s_ring, r_tile, r_usib):
    me = lax.axis_index("prow")
    yy = lax.axis_index("pcol")
    core = me % 2
    chip = me // 2
    x = chip // NZ
    z = chip % NZ

    def tile_of(xx, zz):
        return (zz + NZ - 1) % NZ * NX + (xx + NX - 1) % NX

    def at(xx, zz, cc):
        return {"prow": (xx * NZ + zz) * 2 + cc, "pcol": yy}

    def peer(dchip):
        return {"prow": dchip * 2 + core, "pcol": yy}

    sibling = at(x, z, 1 - core)
    jt = tile_of(x, z)
    holder = jt < TILES

    def remote(src, dst, ss, rs, dev):
        return pltpu.make_async_remote_copy(src_ref=src, dst_ref=dst, send_sem=ss, recv_sem=rs, device_id=dev, device_id_type=MESH)

    def drain(ref, sem):
        pltpu.make_async_copy(ref, ref, sem).wait()

    barrier = pltpu.get_barrier_semaphore()

    def greet(k, _):
        pl.semaphore_signal(barrier, inc=1, device_id=peer((chip + k) % CHIPS), device_id_type=MESH)
        return 0

    lax.fori_loop(1, CHIPS, greet, 0)
    pl.semaphore_signal(barrier, inc=1, device_id=sibling, device_id_type=MESH)
    for k in range(1, NY):
        pl.semaphore_signal(barrier, inc=1, device_id={"prow": me, "pcol": (yy + k) % NY}, device_id_type=MESH)
    pl.semaphore_wait(barrier, CHIPS - 1 + 1 + NY - 1)

    def send_new(k, _):
        d = (chip + k) % CHIPS
        j = tile_of(d // NZ, d % NZ)

        @pl.when(j < TILES)
        def _():
            remote(
                comp.at[:, pl.ds(pl.multiple_of(j * 128, 128), 128)],
                nr.at[pl.ds(pl.multiple_of(chip * CAP, CAP), CAP), :],
                s_nr, r_nr, peer(d),
            ).start()

        return 0

    lax.fori_loop(1, CHIPS, send_new, 0)

    @pl.when(holder)
    def _():
        pltpu.make_async_copy(
            comp.at[:, pl.ds(pl.multiple_of(jt * 128, 128), 128)],
            nr.at[pl.ds(pl.multiple_of(chip * CAP, CAP), CAP), :],
            r_nr,
        ).start()

    for k in range(1, NY):
        dev = {"prow": me, "pcol": (yy + k) % NY}
        remote(inv, invf.at[yy], s_y.at[0], r_inv, dev).start()
        remote(lp, lg.at[yy], s_y.at[1], r_lp, dev).start()
    pltpu.make_async_copy(inv, invf.at[yy], r_inv).start()
    pltpu.make_async_copy(lp, lg.at[yy], r_lp).start()

    @pl.when(chip == 0)
    def _():
        def send_orig(k, _):
            j = tile_of(k // NZ, k % NZ)

            @pl.when(j < TILES)
            def _():
                remote(
                    mat.at[pl.ds(0, BLOCK), pl.ds(pl.multiple_of(j * 128, 128), 128)],
                    orig.at[pl.ds(pl.multiple_of(core * BLOCK, BLOCK), BLOCK), :],
                    s_or, r_or, peer(k),
                ).start()

            return 0

        lax.fori_loop(1, CHIPS, send_orig, 0)

    nr[pl.ds(CHIPS * CAP, 8), :] = jnp.zeros((8, 128), f32)

    my_half = pl.ds(pl.multiple_of(core * BLOCK, BLOCK), BLOCK)
    other_half = pl.ds(pl.multiple_of((1 - core) * BLOCK, BLOCK), BLOCK)

    drain(invf, r_inv)

    @pl.when(holder)
    def _():
        drain(nr.at[pl.ds(0, CHIPS * CAP), :], r_nr)

        def arrange(b, _):
            for t in range(8):
                i = b * 8 + t
                top[pl.ds(i, 1), :] = nr[pl.ds(tab[0, i], 1), :]
            return 0

        lax.fori_loop(0, NB // 8, arrange, 0)
        full = invf[...].reshape(NB, NB)
        top[...] = jnp.dot(full, top[...], precision=lax.Precision.HIGHEST, preferred_element_type=f32)
        back = remote(top.at[other_half, :], psib, s_sib.at[0], r_psib, sibling)
        back.start()
        back.wait()
        u[jt, my_half, :] = top[my_half, :] + psib[...]

    @pl.when(jnp.logical_not(holder))
    def _():
        u[jt, my_half, :] = jnp.zeros((BLOCK, 128), f32)

    def rows_of(part):
        if part is None:
            return my_half
        return pl.ds(pl.multiple_of(core * BLOCK + part * 64, 64), 64)

    def push(xx, zz, part, tx, tz):
        j = tile_of(xx, zz)
        ref = u.at[j, rows_of(part), :]
        remote(ref, ref, s_ring, r_tile.at[j], at(tx, tz, core)).start()

    def share(xx, zz):
        j = tile_of(xx, zz)
        ref = u.at[j, my_half, :]
        remote(ref, ref, s_sib.at[1], r_usib, sibling).start()

    def arrived(xx, zz):
        j = tile_of(xx, zz)
        drain(u.at[j, my_half, :], r_tile.at[j])

    xp, xm = (x + 1) % NX, (x + NX - 1) % NX
    zp, zm = (z + 1) % NZ, (z + NZ - 1) % NZ

    def give_back():
        @pl.when(holder)
        def _():
            drain(orig.at[my_half, :], r_or)
            ref = orig.at[my_half, :]
            copy = remote(ref, ref, s_sib.at[2], r_osib, sibling)
            copy.start()
            copy.wait()

            def arrange(b, _):
                for t in range(8):
                    i = b * 8 + t
                    ret[pl.ds(i, 1), :] = orig[pl.ds(tab[1, i], 1), :]
                return 0

            lax.fori_loop(0, CHIPS * CAP // 8, arrange, 0)

            def send(k, _):
                d = (chip + k) % CHIPS
                remote(ret.at[pl.ds(pl.multiple_of(d * CAP, CAP), CAP), :], sw.at[jt], s_ret, r_ret, peer(d)).start()
                return 0

            lax.fori_loop(1, CHIPS, send, 0)
            pltpu.make_async_copy(ret.at[pl.ds(pl.multiple_of(chip * CAP, CAP), CAP), :], sw.at[jt], r_ret).start()

    def x_neighbours(zz):
        arrived(xm, zz)
        push(xm, zz, 0, xp, z)
        share(xm, zz)
        arrived(xp, zz)
        push(xp, zz, 1, xm, z)
        share(xp, zz)

    def x_far(zz):
        arrived((x + 2) % NX, zz)
        share((x + 2) % NX, zz)

    def z_step(xx, s, onward):
        for sign in (1, -1):
            zz = (z - sign * s + NZ) % NZ
            if s == NZ // 2 and sign == -1:
                continue
            arrived(xx, zz)
            if s < NZ // 2 - 1:
                push(xx, zz, None, x, (z + sign + NZ) % NZ)
            elif s == NZ // 2 - 1:
                push(xx, zz, 0 if sign == 1 else 1, x, (z + sign + NZ) % NZ)
            if onward:
                push(xx, zz, None, xp, z)
                push(xx, zz, None, xm, z)
            share(xx, zz)

    push(x, z, None, x, zp)
    push(x, z, None, x, zm)
    push(x, z, None, xp, z)
    push(x, z, None, xm, z)
    share(x, z)

    @pl.when(core == 0)
    def _():
        def zs(s):
            return [z] if s == 0 else [(z + NZ - s) % NZ] if s == NZ // 2 else [(z + NZ - s) % NZ, (z + s) % NZ]

        for s in range(1, NZ // 2 + 3):
            if s <= NZ // 2:
                z_step(x, s, True)
            if s - 1 <= NZ // 2:
                for zz in zs(s - 1):
                    x_neighbours(zz)
            if s - 2 >= 0:
                for zz in zs(s - 2):
                    x_far(zz)
            if s == 3:
                give_back()

    @pl.when(core == 1)
    def _():
        arrived(xm, z)
        push(xm, z, 0, xp, z)
        push(xm, z, None, x, zp)
        push(xm, z, None, x, zm)
        share(xm, z)
        arrived(xp, z)
        push(xp, z, 1, xm, z)
        push(xp, z, None, x, zp)
        push(xp, z, None, x, zm)
        share(xp, z)
        xf = (x + 2) % NX
        arrived(xf, z)
        push(xf, z, None, x, zp)
        push(xf, z, None, x, zm)
        share(xf, z)
        for s in range(1, NZ // 2 + 1):
            for xx in (x, xm, xp, xf):
                z_step(xx, s, False)
            if s == 2:
                give_back()

    drain(lg, r_lp)
    drain(sw.at[pl.ds(0, TILES)], r_ret)
    drain(u.at[pl.ds(0, CHIPS), other_half, :], r_usib)
    drain(u.at[pl.ds(0, CHIPS), my_half, :], s_sib.at[1])
    drain(u.at[pl.ds(0, CHIPS - 1), my_half, :], s_ring)
    drain(invf.at[pl.ds(0, NY - 1)], s_y.at[0])
    drain(lg.at[pl.ds(0, NY - 1)], s_y.at[1])

    @pl.when(holder)
    def _():
        drain(nr.at[pl.ds(0, (TILES - 1) * CAP), :], s_nr)
        drain(ret.at[pl.ds(0, (CHIPS - 1) * CAP), :], s_ret)

    @pl.when(jnp.logical_not(holder))
    def _():
        drain(nr.at[pl.ds(0, TILES * CAP), :], s_nr)

    @pl.when(chip == 0)
    def _():
        drain(mat.at[pl.ds(0, BLOCK), :], s_or)


def move(tab, comp, matrix, lower_panel, inverse):
    vm = pl.BlockSpec(memory_space=pltpu.VMEM)
    dma = pltpu.SemaphoreType.DMA
    return pl.pallas_call(
        move_kernel,
        out_shape=(
            jax.ShapeDtypeStruct((CHIPS, NB, 128), f32),
            jax.ShapeDtypeStruct((CHIPS, CAP, 128), f32),
            jax.ShapeDtypeStruct((NY, ROWS // NY, NB), f32),
        ),
        in_specs=[pl.BlockSpec(memory_space=pltpu.SMEM), vm, pl.BlockSpec(memory_space=pl.ANY), vm, vm],
        out_specs=(vm, vm, vm),
        scratch_shapes=[
            pltpu.VMEM((CHIPS * CAP + 8, 128), f32),
            pltpu.VMEM((NB, 128), f32),
            pltpu.VMEM((BLOCK, 128), f32),
            pltpu.VMEM((NY, NB // NY, NB), f32),
            pltpu.VMEM((NB, 128), f32),
            pltpu.VMEM((CHIPS * CAP, 128), f32),
            dma, dma, dma, dma, dma((2,)), dma, dma, dma((3,)), dma, dma, dma, dma, dma, dma((CHIPS,)), dma,
        ],
        compiler_params=pltpu.CompilerParams(collective_id=0, has_side_effects=True, vmem_limit_bytes=32 << 20),
        name="move",
    )(tab, comp, matrix, lower_panel, inverse)


def split(v):
    hi = v.astype(bf16)
    return hi, (v - hi.astype(f32)).astype(bf16)


def update_kernel(tab, mat, u, sw, lg, out, l_hi, l_lo, lu):
    me = lax.axis_index("prow")

    @pl.when(pl.program_id(0) == 0)
    def _():
        hi, lo = split(lg[...])
        l_hi[...] = hi
        l_lo[...] = lo

    uu = jnp.concatenate([u[k] for k in range(NX)], axis=1)
    u_hi, u_lo = split(uu)
    prod = functools.partial(jnp.dot, preferred_element_type=f32)
    lu[...] = prod(l_hi[...], u_hi) + (prod(l_lo[...], u_hi) + prod(l_hi[...], u_lo))
    out[...] = mat[...] - lu[...]
    for k in range(CAP):
        row = tab[3, k]

        @pl.when(row >= 0)
        def _():
            new = jnp.concatenate([sw[t, k : k + 1, :] for t in range(NX)], axis=1)
            out[pl.ds(row, 1), :] = new - lu[pl.ds(row, 1), :]

    for half in range(2):

        @pl.when(me == half)
        def _():
            out[0:BLOCK, :] = jnp.concatenate([u[k, half * BLOCK : (half + 1) * BLOCK, :] for k in range(NX)], axis=1)


def update(tab, matrix, u, sw, lg):
    width = NX * 128
    return pl.pallas_call(
        update_kernel,
        grid=(NZ,),
        out_shape=jax.ShapeDtypeStruct((ROWS, COLS), f32),
        in_specs=[
            pl.BlockSpec(memory_space=pltpu.SMEM),
            pl.BlockSpec((ROWS, width), lambda g: (0, g)),
            pl.BlockSpec((NX, NB, 128), lambda g: (g, 0, 0)),
            pl.BlockSpec((NX, CAP, 128), lambda g: (g, 0, 0)),
            pl.BlockSpec((ROWS, NB), lambda g: (0, 0)),
        ],
        out_specs=pl.BlockSpec((ROWS, width), lambda g: (0, g)),
        scratch_shapes=[pltpu.VMEM((ROWS, NB), bf16), pltpu.VMEM((ROWS, NB), bf16), pltpu.VMEM((ROWS, width), f32)],
        compiler_params=pltpu.CompilerParams(vmem_limit_bytes=32 << 20),
        name="update",
    )(tab, matrix, u, sw, lg)


def general(matrix, lg, inverse, source, moved):
    my_row = lax.axis_index("prow")
    row_count = lax.axis_size("prow")
    high = functools.partial(jnp.dot, precision=lax.Precision.HIGHEST, preferred_element_type=f32)
    local_rows = jnp.arange(ROWS, dtype=i32)
    global_rows = (local_rows // BLOCK * row_count + my_row) * BLOCK + local_rows % BLOCK
    owner = source // BLOCK % row_count
    local_index = source // BLOCK // row_count * BLOCK + source % BLOCK
    new_part = jnp.where((owner == my_row)[:, None], jnp.take(matrix, local_index, axis=0), 0.0)
    block_ids = jnp.arange(NB // BLOCK, dtype=i32)
    orig_part = jnp.where((block_ids == my_row)[:, None, None], matrix[None, :BLOCK], 0.0).reshape(NB, COLS)
    gathered, top_orig = lax.psum((new_part, orig_part), "prow")
    hit = (source[None, :] == global_rows[:, None]) & (global_rows >= NB)[:, None]
    fetch = jnp.max(jnp.where(hit, moved[None, :], -1), axis=1)
    swapped = jnp.where((fetch >= 0)[:, None], jnp.take(top_orig, jnp.clip(fetch, 0, NB - 1), axis=0), matrix)
    u_rows = high(lax.all_gather(inverse, "pcol", axis=0, tiled=True), gathered)
    result = swapped - high(lg, u_rows)
    head = lax.dynamic_slice_in_dim(u_rows, jnp.minimum(my_row, 1) * BLOCK, BLOCK, 0)
    first = jnp.where(my_row < 2, head, result[:BLOCK])
    return jnp.concatenate([first, result[BLOCK:]], axis=0)


def local(matrix, lower_panel, inverse, pivots):
    tab, comp = plan(pivots, matrix)
    u, sw, lg = move(tab, comp, matrix, lower_panel, inverse)
    lg = lg.reshape(ROWS, NB)
    return lax.cond(
        tab[6, 0] == 0,
        lambda: update(tab, matrix, u, sw, lg),
        lambda: general(matrix, lg, inverse, tab[4, :NB], tab[5, :NB]),
    )


def solution(mesh):
    return jax.shard_map(
        local,
        mesh=mesh,
        in_specs=(P("prow", "pcol"), P(("prow", "pcol"), None), P("pcol", None), P()),
        out_specs=P("prow", "pcol"),
        check_vma=False,
    )
```

time: 1870 us -> 96 us (0.05); the launches traced: 1850 us -> 95.6 us
  loops' own time: 909 us -> 0.24 us
  other arithmetic: 383 us -> 0 us
  local copies, waits for them, and re-layouts: 324 us -> 3.8 us
  waiting for transfers between devices: 183 us -> 0 us
  Pallas kernels: 0 us -> 77.5 us
  blocking collectives: 22.2 us -> 0 us
    another operation x1, loops' own time: 909 us -> 0.24 us  [local(): lax.cond(tab[6, 0] == 0, lambda: update(tab, matrix, u, sw, lg), lambda:...]
    scatter x512 -> x0, other arithmetic: 372 us -> none  [the longest x256 186 us: turn(): content = content.at[first_slot].set(second_val)]
    psum x1 -> x0, waiting for transfers between devices: 183 us -> none  [local(): gathered = lax.psum(new_part, 'prow')]
    dynamic_slice x256 -> x0, local copies, waits for them, and re-layouts: 152 us -> none  [turn(): second_slot = canonical[panel_width + turn_index]]
    another operation x256 -> x0, local copies, waits for them, and re-layouts: 148 us -> none
    pallas_call x0 -> x3, Pallas kernels: none -> 77.5 us  [the longest x1 65.2 us: move(): pl.pallas_call(move_kernel, out_shape=(jax.ShapeDtypeStruct((CHIPS, NB, 1...]
    gather x3 -> x0, local copies, waits for them, and re-layouts: 22.7 us -> none  [the longest x1 10.1 us: local(): jnp.take(top_orig, jnp.clip(source, 0, panel_width - 1), axis=0)]
    all_gather x2 -> x0, blocking collectives: 22.2 us -> none  [the longest x1 11.2 us: local(): lax.all_gather(inverse, 'pcol', axis=0, tiled=True)]
  transfers between devices with their start and end apart: 1 -> 0, of which waited for: 1 -> 0; matrix products, arithmetic and copies ran while one was open for 0% -> 0% of each run, Pallas kernels for 0% -> 0%
where the time goes in v1:
time: 96 us; the launch traced here: 95.6 us
  Pallas kernels  77.5 us (81%)
  between operations  14.1 us (15%)
  local copies, waits for them, and re-layouts  3.8 us (4%)
    pallas_call x1, Pallas kernels, move(): pl.pallas_call(move_kernel, out_shape=(jax.ShapeDtypeStruct((CHIPS, NB, 1...  65.2 us
    pallas_call x1, Pallas kernels, update(): pl.pallas_call(update_kernel, grid=(NZ,), out_shape=jax.ShapeDtypeStruct(...  9.23 us
    unnamed x8, local copies, waits for them, and re-layouts  3.29 us
    pallas_call x1, Pallas kernels, plan(): pl.pallas_call(plan_kernel, out_shape=(jax.ShapeDtypeStruct((8, 512), i32...  3.11 us

profile of v1, /device:TPU:1, one launch (start us, length us, event | category | flops | bytes accessed | tf_op | source)
XLA Modules:
  0.0 95.6 jit_solution(671546690998948400)
XLA Ops:
  6.5 0.0 copy-start
  6.5 0.0 copy-start.1
  6.5 0.7 copy-done.1
  7.3 0.0 copy-start.4
  7.3 3.1 %plan.1 = (s32[8,512]{1,0:T(8,128)S(1)}, f32[16,3840]{1,0:T(8,128)S(1)}) custom-call(s32[1,256]{1,0:T(1,128)S(1)} %bitcast.35, f32[384,3840]{1,0:T(8,128)} %mat.3), custom_call_target="tpu_custom_call" | custom-call | tf_op jit(solution)/shard_map/plan/pallas_call | solution.py:108
  10.4 0.0 copy-done
  10.4 0.0 copy-done.4
  10.4 65.2 %move.1 = (f32[32,256,128]{2,1,0:T(8,128)}, f32[32,16,128]{2,1,0:T(8,128)S(1)}, f32[4,96,256]{2,1,0:T(8,128)S(1)}) custom-call(s32[8,512]{1,0:T(8,128)S(1)} %get-tuple-element.40.tab, f32[16,3840]{1,0:T(8,128)S(1)} %get-tuple-element.41.comp, f32[384,3840]{1,0:T(8,128)} %mat.3, f32[96,256]{1,0:T(8,128)S(1)} %copy-done, f32[64,256]{1,0:T(8,128)S(1)} %copy-done.4), custom_call_target="tpu_custom_call" | custom-call | tf_op jit(solution)/shard_map/move/pallas_call | solution.py:385
  75.6 0.5 slice.18
  76.7 9.5 %conditional.1 = (f32[384,3840]{1,0:T(8,128)S(1)}) conditional(s32[]{:T(128)} %bitcast.9, (s32[8,512]{1,0:T(8,128)S(1)}, f32[384,3840]{1,0:T(8,128)}, f32[64,256]{1,0:T(8,128)S(1)}, f32[384,256]{1,0:T(8,128)S(1)}) %tuple.27, (s32[8,512]{1,0:T(8,128)S(1)}, f32[384,3840]{1,0:T(8,128)}, f32[32,256,128]{2,1,0:T(8,128)}, f32[32,16,128]{2,1,0:T(8,128)S(1)}, ...), branch_computations={%region_0.4_spmd, %region_4.5_spmd} | conditional | flops 7561489920 | bytes 164209600 | solution.py:488
  77.0 9.2 %update.1 = f32[384,3840]{1,0:T(8,128)S(1)} custom-call(s32[8,512]{1,0:T(8,128)S(1)} %get-tuple-element.30.tab, f32[384,3840]{1,0:T(8,128)} %get-tuple-element.31.mat, f32[32,256,128]{2,1,0:T(8,128)} %get-tuple-element.32.u, f32[32,16,128]{2,1,0:T(8,128)S(1)} %get-tuple-element.33.sw, f32[384,256]{1,0:T(8,128)S(1)} %get-tuple-element.34.lg), custom_call_target="tpu_custom_call" | custom-call | tf_op jit(solution)/shard_map/cond/branch_1_fun/update/pallas_call | solution.py:444
  86.2 0.0 copy-start.3
  86.2 2.6 %copy-done.3 = f32[384,3840]{1,0:T(8,128)} copy-done((f32[384,3840]{1,0:T(8,128)}, f32[384,3840]{1,0:T(8,128)S(1)}, u32[]{:S(2)}) %copy-start.3) | copy-done | bytes 5898264
Async XLA Ops:
  6.5 3.8 %copy-start = (f32[96,256]{1,0:T(8,128)S(1)}, f32[96,256]{1,0:T(8,128)}, u32[]{:S(2)}) copy-start(f32[96,256]{1,0:T(8,128)} %lp.1) | copy-start | bytes 294916
  6.5 0.7 copy-start.1
  7.3 3.1 %copy-start.4 = (f32[64,256]{1,0:T(8,128)S(1)}, f32[64,256]{1,0:T(8,128)}, u32[]{:S(2)}) copy-start(f32[64,256]{1,0:T(8,128)} %inv.1) | copy-start | bytes 196612
  86.2 2.6 %copy-start.3 = (f32[384,3840]{1,0:T(8,128)}, f32[384,3840]{1,0:T(8,128)S(1)}, u32[]{:S(2)}) copy-start(f32[384,3840]{1,0:T(8,128)S(1)} %get-tuple-element.67) | copy-start | bytes 17694724

commit v2 on v1

--- a/solution.py
+++ b/solution.py
@@ -11,7 +11,9 @@
 NB = 256
 CAP = 16
 NX, NZ, NY = 4, 8, 4
+N_PROW = 64
 CHIPS = NX * NZ
+AWAY = (4, 3, 5, 2, 6, 1, 7)
 TILES = 30
 COLS = TILES * 128
 ROWS = 384
@@ -115,13 +117,14 @@
             pltpu.SemaphoreType.DMA,
             pltpu.SemaphoreType.DMA((CAP,)),
         ],
-        compiler_params=pltpu.CompilerParams(vmem_limit_bytes=24 << 20),
+        compiler_params=pltpu.CompilerParams(vmem_limit_bytes=16 << 20),
         name="plan",
     )(pivots.reshape(1, NB), matrix)
 
 
 def move_kernel(tab, comp, mat, lp, inv, u, sw, lg, nr, top, psib, invf, orig, ret,
-                s_nr, r_nr, s_or, r_or, s_y, r_inv, r_lp, s_sib, r_psib, r_osib, s_ret, r_ret, s_ring, r_tile, r_usib):
+                s_nr, r_nr, s_or, r_or, s_y, r_inv, r_lp, s_sib, r_psib, r_osib, s_ret, r_ret, s_ring, r_tile, r_usib,
+                relay, s_relay, r_relay):
     me = lax.axis_index("prow")
     yy = lax.axis_index("pcol")
     core = me % 2
@@ -138,6 +141,8 @@
     def peer(dchip):
         return {"prow": dchip * 2 + core, "pcol": yy}
 
+    my_half = pl.ds(pl.multiple_of(core * BLOCK, BLOCK), BLOCK)
+    other_half = pl.ds(pl.multiple_of((1 - core) * BLOCK, BLOCK), BLOCK)
     sibling = at(x, z, 1 - core)
     jt = tile_of(x, z)
     holder = jt < TILES
@@ -160,8 +165,16 @@
         pl.semaphore_signal(barrier, inc=1, device_id={"prow": me, "pcol": (yy + k) % NY}, device_id_type=MESH)
     pl.semaphore_wait(barrier, CHIPS - 1 + 1 + NY - 1)
 
+    for k in range(1, NY):
+        remote(inv, invf.at[yy], s_y.at[0], r_inv, {"prow": me, "pcol": (yy + k) % NY}).start()
+    pltpu.make_async_copy(inv, invf.at[yy], r_inv).start()
+
+    def spread(k):
+        k = k * 13 % CHIPS
+        return (x + k // NZ) % NX * NZ + (z + k) % NZ
+
     def send_new(k, _):
-        d = (chip + k) % CHIPS
+        d = spread(k)
         j = tile_of(d // NZ, d % NZ)
 
         @pl.when(j < TILES)
@@ -184,34 +197,28 @@
             r_nr,
         ).start()
 
+    @pl.when(chip == 0)
+    def _():
+        def send_orig(xx, zz, dst, sem, to):
+            cols = pl.ds(tile_of(xx, zz) * 128, 128)
+            remote(mat.at[pl.ds(0, BLOCK), cols], dst, s_or, sem, to).start()
+
+        mine = orig.at[my_half, :]
+        send_orig(1, 0, mine, r_or, at(1, 0, core))
+        send_orig(2, 0, relay.at[0], r_relay.at[0], at(3, 0, core))
+        for zz in AWAY:
+            send_orig(1, zz, relay.at[zz], r_relay.at[zz], at(1, 0, core))
+            send_orig(3, zz, relay.at[zz], r_relay.at[zz], at(3, 0, core))
+            send_orig(2, zz, mine, r_or, at(2, zz, core))
+        for zz in AWAY:
+            send_orig(0, zz, mine, r_or, at(0, zz, core))
+
     for k in range(1, NY):
-        dev = {"prow": me, "pcol": (yy + k) % NY}
-        remote(inv, invf.at[yy], s_y.at[0], r_inv, dev).start()
-        remote(lp, lg.at[yy], s_y.at[1], r_lp, dev).start()
-    pltpu.make_async_copy(inv, invf.at[yy], r_inv).start()
+        remote(lp, lg.at[yy], s_y.at[1], r_lp, {"prow": me, "pcol": (yy + k) % NY}).start()
     pltpu.make_async_copy(lp, lg.at[yy], r_lp).start()
 
-    @pl.when(chip == 0)
-    def _():
-        def send_orig(k, _):
-            j = tile_of(k // NZ, k % NZ)
-
-            @pl.when(j < TILES)
-            def _():
-                remote(
-                    mat.at[pl.ds(0, BLOCK), pl.ds(pl.multiple_of(j * 128, 128), 128)],
-                    orig.at[pl.ds(pl.multiple_of(core * BLOCK, BLOCK), BLOCK), :],
-                    s_or, r_or, peer(k),
-                ).start()
-
-            return 0
-
-        lax.fori_loop(1, CHIPS, send_orig, 0)
-
     nr[pl.ds(CHIPS * CAP, 8), :] = jnp.zeros((8, 128), f32)
 
-    my_half = pl.ds(pl.multiple_of(core * BLOCK, BLOCK), BLOCK)
-    other_half = pl.ds(pl.multiple_of((1 - core) * BLOCK, BLOCK), BLOCK)
 
     drain(invf, r_inv)
 
@@ -256,7 +263,7 @@
         j = tile_of(xx, zz)
         drain(u.at[j, my_half, :], r_tile.at[j])
 
-    xp, xm = (x + 1) % NX, (x + NX - 1) % NX
+    xp, xm, xf = (x + 1) % NX, (x + NX - 1) % NX, (x + 2) % NX
     zp, zm = (z + 1) % NZ, (z + NZ - 1) % NZ
 
     def give_back():
@@ -277,7 +284,7 @@
             lax.fori_loop(0, CHIPS * CAP // 8, arrange, 0)
 
             def send(k, _):
-                d = (chip + k) % CHIPS
+                d = spread(k)
                 remote(ret.at[pl.ds(pl.multiple_of(d * CAP, CAP), CAP), :], sw.at[jt], s_ret, r_ret, peer(d)).start()
                 return 0
 
@@ -293,10 +300,10 @@
         share(xp, zz)
 
     def x_far(zz):
-        arrived((x + 2) % NX, zz)
-        share((x + 2) % NX, zz)
-
-    def z_step(xx, s, onward):
+        arrived(xf, zz)
+        share(xf, zz)
+
+    def z_step(xx, s):
         for sign in (1, -1):
             zz = (z - sign * s + NZ) % NZ
             if s == NZ // 2 and sign == -1:
@@ -306,55 +313,88 @@
                 push(xx, zz, None, x, (z + sign + NZ) % NZ)
             elif s == NZ // 2 - 1:
                 push(xx, zz, 0 if sign == 1 else 1, x, (z + sign + NZ) % NZ)
-            if onward:
-                push(xx, zz, None, xp, z)
-                push(xx, zz, None, xm, z)
             share(xx, zz)
 
     push(x, z, None, x, zp)
     push(x, z, None, x, zm)
     push(x, z, None, xp, z)
     push(x, z, None, xm, z)
+
+    @pl.when(core == 0)
+    def _():
+        push(x, z, None, x, (z + 2) % NZ)
+        push(x, z, None, x, (z + NZ - 2) % NZ)
+
+    @pl.when(core == 1)
+    def _():
+        push(x, z, None, xf, z)
+
     share(x, z)
 
+    def hand_on(zz):
+        @pl.when((z == 0) & ((x == 3) | ((x == 1) & (zz > 0))))
+        def _():
+            drain(relay.at[zz], r_relay.at[zz])
+            to = at(x, zz, core) if zz > 0 else at(2, 0, core)
+            remote(relay.at[zz], orig.at[my_half, :], s_relay, r_or, to).start()
+
+    hand_on(0)
+    for zz in AWAY[:3]:
+        hand_on(zz)
+
+    def back(s):
+        return (z + NZ - s) % NZ
+
+    def onward(zz):
+        push(x, zz, None, xp, z)
+        push(x, zz, None, xm, z)
+        share(x, zz)
+
     @pl.when(core == 0)
     def _():
-        def zs(s):
-            return [z] if s == 0 else [(z + NZ - s) % NZ] if s == NZ // 2 else [(z + NZ - s) % NZ, (z + s) % NZ]
-
-        for s in range(1, NZ // 2 + 3):
-            if s <= NZ // 2:
-                z_step(x, s, True)
-            if s - 1 <= NZ // 2:
-                for zz in zs(s - 1):
-                    x_neighbours(zz)
-            if s - 2 >= 0:
-                for zz in zs(s - 2):
-                    x_far(zz)
-            if s == 3:
-                give_back()
+        for s in (2, -2):
+            arrived(x, back(s))
+            push(x, back(s), None, x, back(-s // 2))
+            push(x, back(s), 0 if s > 0 else 1, x, back(-s))
+            onward(back(s))
+        for s in (1, -1):
+            arrived(x, back(s))
+            onward(back(s))
+        for zz in AWAY[3:]:
+            hand_on(zz)
+        x_neighbours(z)
+        for s in (3, -3):
+            arrived(x, back(s))
+            onward(back(s))
+        for s in (2, -2):
+            x_neighbours(back(s))
+        arrived(x, back(4))
+        onward(back(4))
+        give_back()
+        for s in (1, -1):
+            x_neighbours(back(s))
+        x_far(z)
+        for s in (3, -3):
+            x_neighbours(back(s))
+        for s in (2, -2, 1, -1):
+            x_far(back(s))
+        x_neighbours(back(4))
+        for s in (3, -3, 4):
+            x_far(back(s))
 
     @pl.when(core == 1)
     def _():
-        arrived(xm, z)
-        push(xm, z, 0, xp, z)
-        push(xm, z, None, x, zp)
-        push(xm, z, None, x, zm)
-        share(xm, z)
-        arrived(xp, z)
-        push(xp, z, 1, xm, z)
-        push(xp, z, None, x, zp)
-        push(xp, z, None, x, zm)
-        share(xp, z)
-        xf = (x + 2) % NX
-        arrived(xf, z)
-        push(xf, z, None, x, zp)
-        push(xf, z, None, x, zm)
-        share(xf, z)
+        for xx in (xm, xp, xf):
+            arrived(xx, z)
+            push(xx, z, None, x, zp)
+            push(xx, z, None, x, zm)
+            share(xx, z)
+        for zz in AWAY[3:]:
+            hand_on(zz)
         for s in range(1, NZ // 2 + 1):
             for xx in (x, xm, xp, xf):
-                z_step(xx, s, False)
-            if s == 2:
+                z_step(xx, s)
+            if s == 1:
                 give_back()
 
     drain(lg, r_lp)
@@ -373,6 +413,14 @@
     @pl.when(jnp.logical_not(holder))
     def _():
         drain(nr.at[pl.ds(0, TILES * CAP), :], s_nr)
+
+    @pl.when((z == 0) & (x == 1))
+    def _():
+        drain(relay.at[pl.ds(1, NZ - 1)], s_relay)
+
+    @pl.when((z == 0) & (x == 3))
+    def _():
+        drain(relay, s_relay)
 
     @pl.when(chip == 0)
     def _():
@@ -399,8 +447,9 @@
             pltpu.VMEM((NB, 128), f32),
             pltpu.VMEM((CHIPS * CAP, 128), f32),
             dma, dma, dma, dma, dma((2,)), dma, dma, dma((3,)), dma, dma, dma, dma, dma, dma((CHIPS,)), dma,
+            pltpu.VMEM((NZ, BLOCK, 128), f32), dma, dma((NZ,)),
         ],
-        compiler_params=pltpu.CompilerParams(collective_id=0, has_side_effects=True, vmem_limit_bytes=32 << 20),
+        compiler_params=pltpu.CompilerParams(collective_id=0, has_side_effects=True, vmem_limit_bytes=16 << 20),
         name="move",
     )(tab, comp, matrix, lower_panel, inverse)
 
@@ -454,9 +503,17 @@
         ],
         out_specs=pl.BlockSpec((ROWS, width), lambda g: (0, g)),
         scratch_shapes=[pltpu.VMEM((ROWS, NB), bf16), pltpu.VMEM((ROWS, NB), bf16), pltpu.VMEM((ROWS, width), f32)],
-        compiler_params=pltpu.CompilerParams(vmem_limit_bytes=32 << 20),
+        compiler_params=pltpu.CompilerParams(vmem_limit_bytes=16 << 20),
         name="update",
     )(tab, matrix, u, sw, lg)
+
+
+def total(value, axis, size):
+    step = 1
+    while step < size:
+        value = value + lax.ppermute(value, axis, [(i, i ^ step) for i in range(size)])
+        step *= 2
+    return value
 
 
 def general(matrix, lg, inverse, source, moved):
@@ -470,11 +527,12 @@
     new_part = jnp.where((owner == my_row)[:, None], jnp.take(matrix, local_index, axis=0), 0.0)
     block_ids = jnp.arange(NB // BLOCK, dtype=i32)
     orig_part = jnp.where((block_ids == my_row)[:, None, None], matrix[None, :BLOCK], 0.0).reshape(NB, COLS)
-    gathered, top_orig = lax.psum((new_part, orig_part), "prow")
+    gathered, top_orig = jnp.split(total(jnp.concatenate([new_part, orig_part]), "prow", N_PROW), 2)
     hit = (source[None, :] == global_rows[:, None]) & (global_rows >= NB)[:, None]
     fetch = jnp.max(jnp.where(hit, moved[None, :], -1), axis=1)
     swapped = jnp.where((fetch >= 0)[:, None], jnp.take(top_orig, jnp.clip(fetch, 0, NB - 1), axis=0), matrix)
-    u_rows = high(lax.all_gather(inverse, "pcol", axis=0, tiled=True), gathered)
+    parts = jnp.where((jnp.arange(NY) == lax.axis_index("pcol"))[:, None, None], inverse[None], 0.0)
+    u_rows = high(total(parts.reshape(NB, NB), "pcol", NY), gathered)
     result = swapped - high(lg, u_rows)
     head = lax.dynamic_slice_in_dim(u_rows, jnp.minimum(my_row, 1) * BLOCK, BLOCK, 0)
     first = jnp.where(my_row < 2, head, result[:BLOCK])
@@ -485,11 +543,13 @@
     tab, comp = plan(pivots, matrix)
     u, sw, lg = move(tab, comp, matrix, lower_panel, inverse)
     lg = lg.reshape(ROWS, NB)
-    return lax.cond(
-        tab[6, 0] == 0,
-        lambda: update(tab, matrix, u, sw, lg),
-        lambda: general(matrix, lg, inverse, tab[4, :NB], tab[5, :NB]),
+    result = update(tab, matrix, u, sw, lg)
+    _, result = lax.while_loop(
+        lambda state: state[0] > 0,
+        lambda state: (jnp.int32(0), general(matrix, lg, inverse, tab[4, :NB], tab[5, :NB])),
+        (tab[6, 0], result),
     )
+    return result
 
 
 def solution(mesh):

time: 96 us -> 67.5 us (0.70)
  between operations: 14.1 us -> 0.23 us
  Pallas kernels: 77.5 us -> 64.9 us
  local copies, waits for them, and re-layouts: 3.8 us -> 1.31 us
    pallas_call x1, Pallas kernels: 65.2 us -> 53.9 us  [move(): pl.pallas_call(move_kernel, out_shape=(jax.ShapeDtypeStruct((CHIPS, NB, 1...]
    unnamed x8 -> x10, local copies, waits for them, and re-layouts: 3.29 us -> 0.73 us
    pallas_call x1, Pallas kernels: 9.23 us -> 7.94 us  [update(): pl.pallas_call(update_kernel, grid=(NZ,), out_shape=jax.ShapeDtypeStruct(...]
where the time goes in v2:
time: 67.5 us; the launch traced here: 67.4 us
  Pallas kernels  64.9 us (96%)
  local copies, waits for them, and re-layouts  1.31 us (2%)
  loops' own time  0.91 us (1%)
    pallas_call x1, Pallas kernels, move(): pl.pallas_call(move_kernel, out_shape=(jax.ShapeDtypeStruct((CHIPS, NB, 1...  53.9 us
    pallas_call x1, Pallas kernels, update(): pl.pallas_call(update_kernel, grid=(NZ,), out_shape=jax.ShapeDtypeStruct(...  7.94 us
    pallas_call x1, Pallas kernels, plan(): pl.pallas_call(plan_kernel, out_shape=(jax.ShapeDtypeStruct((8, 512), i32...  3.11 us

profile of v2, /device:TPU:1, one launch (start us, length us, event | category | flops | bytes accessed | tf_op | source)
XLA Modules:
  0.0 67.4 jit_solution(16757729926149968678)
XLA Ops:
  0.0 0.0 copy-start
  0.0 0.0 copy-start.1
  0.0 0.7 %copy-done.1 = s32[256]{0:T(256)S(1)} copy-done((s32[256]{0:T(256)S(1)}, s32[256]{0:T(256)}, u32[]{:S(2)}) %copy-start.1) | copy-done | bytes 1048
  0.7 0.0 copy-start.2
  0.7 3.1 %plan.1 = (s32[8,512]{1,0:T(8,128)S(1)}, f32[16,3840]{1,0:T(8,128)S(1)}) custom-call(s32[1,256]{1,0:T(1,128)S(1)} %bitcast.33, f32[384,3840]{1,0:T(8,128)} %mat.5), custom_call_target="tpu_custom_call" | custom-call | tf_op jit(solution)/shard_map/plan/pallas_call | solution.py:110
  3.8 0.0 copy-done
  3.8 53.9 %move.1 = (f32[32,256,128]{2,1,0:T(8,128)S(1)}, f32[32,16,128]{2,1,0:T(8,128)S(1)}, f32[4,96,256]{2,1,0:T(8,128)S(1)}) custom-call(s32[8,512]{1,0:T(8,128)S(1)} %get-tuple-element.75.tab, f32[16,3840]{1,0:T(8,128)S(1)} %get-tuple-element.41.comp, f32[384,3840]{1,0:T(8,128)} %mat.5, f32[96,256]{1,0:T(8,128)S(1)} %copy-done, f32[64,256]{1,0:T(8,128)} %inv.1), custom_call_target="tpu_custom_call" | custom-call | tf_op jit(solution)/shard_map/move/pallas_call | solution.py:433
  57.7 0.0 copy-start.7
  57.7 0.0 copy-done.2
  57.7 0.0 copy-start.9
  57.8 7.9 %update.1 = f32[384,3840]{1,0:T(8,128)} custom-call(s32[8,512]{1,0:T(8,128)S(1)} %get-tuple-element.75.tab, f32[384,3840]{1,0:T(8,128)S(1)} %copy-done.2, f32[32,256,128]{2,1,0:T(8,128)S(1)} %get-tuple-element.42.u, f32[32,16,128]{2,1,0:T(8,128)S(1)} %get-tuple-element.43.sw, f32[384,256]{1,0:T(8,128)S(1)} %bitcast.34), custom_call_target="tpu_custom_call" | custom-call | tf_op jit(solution)/shard_map/update/pallas_call | solution.py:493
  65.7 0.0 copy-done.7
  65.7 0.6 slice.18
  66.3 0.0 copy-done.9
  66.3 0.9 %while.9 = (s32[]{:T(128)}, f32[384,3840]{1,0:T(8,128)}, f32[64,256]{1,0:T(8,128)S(1)}, s32[8,512]{1,0:T(8,128)S(1)}, f32[384,3840]{1,0:T(8,128)}, /*index=5*/f32[384,256]{1,0:T(8,128)}) while((s32[]{:T(128)}, f32[384,3840]{1,0:T(8,128)}, f32[64,256]{1,0:T(8,128)S(1)}, s32[8,512]{1,0:T(8,128)S(1)}, f32[384,3840]{1,0:T(8,128)}, ...), condition=%region_2.3_spmd, body=%region_0.2_spmd | while | flops 7575514624 | bytes 526559744 | solution.py:547
Async XLA Ops:
  0.0 3.8 %copy-start = (f32[96,256]{1,0:T(8,128)S(1)}, f32[96,256]{1,0:T(8,128)}, u32[]{:S(2)}) copy-start(f32[96,256]{1,0:T(8,128)} %lp.1) | copy-start | bytes 294916
  0.0 0.7 %copy-start.1 = (s32[256]{0:T(256)S(1)}, s32[256]{0:T(256)}, u32[]{:S(2)}) copy-start(s32[256]{0:T(256)} %param.9) | copy-start | bytes 3076
  0.7 57.0 %copy-start.2 = (f32[384,3840]{1,0:T(8,128)S(1)}, f32[384,3840]{1,0:T(8,128)}, u32[]{:S(2)}) copy-start(f32[384,3840]{1,0:T(8,128)} %mat.5) | copy-start | bytes 17694724
  57.7 8.0 %copy-start.7 = (f32[4,96,256]{2,1,0:T(8,128)}, f32[4,96,256]{2,1,0:T(8,128)S(1)}, u32[]{:S(2)}) copy-start(f32[4,96,256]{2,1,0:T(8,128)S(1)} %get-tuple-element.44) | copy-start | bytes 1179652
  57.7 8.5 %copy-start.9 = (f32[64,256]{1,0:T(8,128)S(1)}, f32[64,256]{1,0:T(8,128)}, u32[]{:S(2)}) copy-start(f32[64,256]{1,0:T(8,128)} %inv.1) | copy-start | bytes 196612

commit v3 on v2

--- a/solution.py
+++ b/solution.py
@@ -13,6 +13,8 @@
 NX, NZ, NY = 4, 8, 4
 N_PROW = 64
 CHIPS = NX * NZ
+STEP = 10
+SHARE = ((0, 112), (112, 144))
 AWAY = (4, 3, 5, 2, 6, 1, 7)
 TILES = 30
 COLS = TILES * 128
@@ -23,7 +25,7 @@
 bf16 = jnp.bfloat16
 
 
-def plan_kernel(p_ref, mat, tab, comp, tab_s, sem, row_sems):
+def plan_kernel(p_ref, mat, tab, comp, crowded, tab_s, sem, row_sems):
     me = lax.axis_index("prow")
     core = (me % 2).astype(f32)
     mef = me.astype(f32)
@@ -91,7 +93,7 @@
     tab[3:4, 0:128] = dest.astype(i32)
     tab[4:5, 0:NB] = to_row(ts).astype(i32)
     tab[5:6, 0:NB] = to_row(w).astype(i32)
-    tab[6:7, 0:128] = jnp.broadcast_to(jnp.where(flag, 1, 0), (1, 128)).astype(i32)
+    crowded[0, 0] = jnp.where(flag, 1, 0)
     copy = pltpu.make_async_copy(tab.at[2:3, 0:128], tab_s, sem)
     copy.start()
     copy.wait()
@@ -109,9 +111,13 @@
     vm = pl.BlockSpec(memory_space=pltpu.VMEM)
     return pl.pallas_call(
         plan_kernel,
-        out_shape=(jax.ShapeDtypeStruct((8, 512), i32), jax.ShapeDtypeStruct((CAP, COLS), f32)),
+        out_shape=(
+            jax.ShapeDtypeStruct((8, 512), i32),
+            jax.ShapeDtypeStruct((CAP, COLS), f32),
+            jax.ShapeDtypeStruct((1, 1), i32),
+        ),
         in_specs=[vm, pl.BlockSpec(memory_space=pl.ANY)],
-        out_specs=(vm, vm),
+        out_specs=(vm, vm, pl.BlockSpec(memory_space=pltpu.SMEM)),
         scratch_shapes=[
             pltpu.SMEM((1, 128), i32),
             pltpu.SemaphoreType.DMA,
@@ -142,7 +148,6 @@
         return {"prow": dchip * 2 + core, "pcol": yy}
 
     my_half = pl.ds(pl.multiple_of(core * BLOCK, BLOCK), BLOCK)
-    other_half = pl.ds(pl.multiple_of((1 - core) * BLOCK, BLOCK), BLOCK)
     sibling = at(x, z, 1 - core)
     jt = tile_of(x, z)
     holder = jt < TILES
@@ -235,45 +240,60 @@
         lax.fori_loop(0, NB // 8, arrange, 0)
         full = invf[...].reshape(NB, NB)
         top[...] = jnp.dot(full, top[...], precision=lax.Precision.HIGHEST, preferred_element_type=f32)
-        back = remote(top.at[other_half, :], psib, s_sib.at[0], r_psib, sibling)
-        back.start()
-        back.wait()
-        u[jt, my_half, :] = top[my_half, :] + psib[...]
-
-    @pl.when(jnp.logical_not(holder))
-    def _():
-        u[jt, my_half, :] = jnp.zeros((BLOCK, 128), f32)
-
-    def rows_of(part):
-        if part is None:
-            return my_half
-        return pl.ds(pl.multiple_of(core * BLOCK + part * 64, 64), 64)
-
-    def push(xx, zz, part, tx, tz):
+
+        def finish(c):
+            own, other = (pl.ds(*SHARE[c]), pl.ds(*SHARE[1 - c]))
+            part = psib.at[pl.ds(0, SHARE[c][1])]
+            out = remote(top.at[other], psib.at[pl.ds(0, SHARE[1 - c][1])], s_sib.at[0], r_psib, sibling)
+            out.start()
+            drain(part, r_psib)
+            u[jt, own, :] = top[own, :] + part[...]
+            out.wait_send()
+
+        pl.when(core == 0)(lambda: finish(0))
+        pl.when(core == 1)(lambda: finish(1))
+
+    for c in range(2):
+
+        @pl.when(jnp.logical_not(holder) & (core == c))
+        def _():
+            u[jt, pl.ds(*SHARE[c]), :] = jnp.zeros((SHARE[c][1], 128), f32)
+
+    def rows_of(c, part=None):
+        start, size = SHARE[c]
+        return pl.ds(start, size) if part is None else pl.ds(start + part * (size // 2), size // 2)
+
+    def push(c, xx, zz, part, tx, tz):
         j = tile_of(xx, zz)
-        ref = u.at[j, rows_of(part), :]
+        ref = u.at[j, rows_of(c, part), :]
         remote(ref, ref, s_ring, r_tile.at[j], at(tx, tz, core)).start()
 
-    def share(xx, zz):
+    def share(c, xx, zz):
         j = tile_of(xx, zz)
-        ref = u.at[j, my_half, :]
+        ref = u.at[j, rows_of(c), :]
         remote(ref, ref, s_sib.at[1], r_usib, sibling).start()
 
-    def arrived(xx, zz):
+    def arrived(c, xx, zz):
         j = tile_of(xx, zz)
-        drain(u.at[j, my_half, :], r_tile.at[j])
+        drain(u.at[j, rows_of(c), :], r_tile.at[j])
 
     xp, xm, xf = (x + 1) % NX, (x + NX - 1) % NX, (x + 2) % NX
     zp, zm = (z + 1) % NZ, (z + NZ - 1) % NZ
 
+    def swap_halves():
+        ref = orig.at[my_half, :]
+        return remote(ref, ref, s_sib.at[2], r_osib, sibling)
+
+    def swap_first():
+        @pl.when(holder)
+        def _():
+            drain(orig.at[my_half, :], r_or)
+            swap_halves().start()
+
     def give_back():
         @pl.when(holder)
         def _():
-            drain(orig.at[my_half, :], r_or)
-            ref = orig.at[my_half, :]
-            copy = remote(ref, ref, s_sib.at[2], r_osib, sibling)
-            copy.start()
-            copy.wait()
+            swap_halves().wait()
 
             def arrange(b, _):
                 for t in range(8):
@@ -292,44 +312,43 @@
             pltpu.make_async_copy(ret.at[pl.ds(pl.multiple_of(chip * CAP, CAP), CAP), :], sw.at[jt], r_ret).start()
 
     def x_neighbours(zz):
-        arrived(xm, zz)
-        push(xm, zz, 0, xp, z)
-        share(xm, zz)
-        arrived(xp, zz)
-        push(xp, zz, 1, xm, z)
-        share(xp, zz)
+        arrived(0, xm, zz)
+        push(0, xm, zz, 0, xp, z)
+        share(0, xm, zz)
+        arrived(0, xp, zz)
+        push(0, xp, zz, 1, xm, z)
+        share(0, xp, zz)
 
     def x_far(zz):
-        arrived(xf, zz)
-        share(xf, zz)
+        arrived(0, xf, zz)
+        share(0, xf, zz)
 
     def z_step(xx, s):
         for sign in (1, -1):
             zz = (z - sign * s + NZ) % NZ
             if s == NZ // 2 and sign == -1:
                 continue
-            arrived(xx, zz)
+            arrived(1, xx, zz)
             if s < NZ // 2 - 1:
-                push(xx, zz, None, x, (z + sign + NZ) % NZ)
+                push(1, xx, zz, None, x, (z + sign + NZ) % NZ)
             elif s == NZ // 2 - 1:
-                push(xx, zz, 0 if sign == 1 else 1, x, (z + sign + NZ) % NZ)
-            share(xx, zz)
-
-    push(x, z, None, x, zp)
-    push(x, z, None, x, zm)
-    push(x, z, None, xp, z)
-    push(x, z, None, xm, z)
-
-    @pl.when(core == 0)
-    def _():
-        push(x, z, None, x, (z + 2) % NZ)
-        push(x, z, None, x, (z + NZ - 2) % NZ)
-
-    @pl.when(core == 1)
-    def _():
-        push(x, z, None, xf, z)
-
-    share(x, z)
+                push(1, xx, zz, 0 if sign == 1 else 1, x, (z + sign + NZ) % NZ)
+            share(1, xx, zz)
+
+    def begin(c):
+        push(c, x, z, None, x, zp)
+        push(c, x, z, None, x, zm)
+        push(c, x, z, None, xp, z)
+        push(c, x, z, None, xm, z)
+        if c == 0:
+            push(c, x, z, None, x, (z + 2) % NZ)
+            push(c, x, z, None, x, (z + NZ - 2) % NZ)
+        else:
+            push(c, x, z, None, xf, z)
+        share(c, x, z)
+
+    pl.when(core == 0)(lambda: begin(0))
+    pl.when(core == 1)(lambda: begin(1))
 
     def hand_on(zz):
         @pl.when((z == 0) & ((x == 3) | ((x == 1) & (zz > 0))))
@@ -346,29 +365,30 @@
         return (z + NZ - s) % NZ
 
     def onward(zz):
-        push(x, zz, None, xp, z)
-        push(x, zz, None, xm, z)
-        share(x, zz)
+        push(0, x, zz, None, xp, z)
+        push(0, x, zz, None, xm, z)
+        share(0, x, zz)
 
     @pl.when(core == 0)
     def _():
         for s in (2, -2):
-            arrived(x, back(s))
-            push(x, back(s), None, x, back(-s // 2))
-            push(x, back(s), 0 if s > 0 else 1, x, back(-s))
+            arrived(0, x, back(s))
+            push(0, x, back(s), None, x, back(-s // 2))
+            push(0, x, back(s), 0 if s > 0 else 1, x, back(-s))
             onward(back(s))
         for s in (1, -1):
-            arrived(x, back(s))
+            arrived(0, x, back(s))
             onward(back(s))
         for zz in AWAY[3:]:
             hand_on(zz)
         x_neighbours(z)
         for s in (3, -3):
-            arrived(x, back(s))
+            arrived(0, x, back(s))
             onward(back(s))
+        swap_first()
         for s in (2, -2):
             x_neighbours(back(s))
-        arrived(x, back(4))
+        arrived(0, x, back(4))
         onward(back(4))
         give_back()
         for s in (1, -1):
@@ -385,23 +405,29 @@
     @pl.when(core == 1)
     def _():
         for xx in (xm, xp, xf):
-            arrived(xx, z)
-            push(xx, z, None, x, zp)
-            push(xx, z, None, x, zm)
-            share(xx, z)
+            arrived(1, xx, z)
+            push(1, xx, z, None, x, zp)
+            push(1, xx, z, None, x, zm)
+            share(1, xx, z)
         for zz in AWAY[3:]:
             hand_on(zz)
         for s in range(1, NZ // 2 + 1):
             for xx in (x, xm, xp, xf):
                 z_step(xx, s)
             if s == 1:
+                swap_first()
+            if s == 2:
                 give_back()
 
     drain(lg, r_lp)
     drain(sw.at[pl.ds(0, TILES)], r_ret)
-    drain(u.at[pl.ds(0, CHIPS), other_half, :], r_usib)
-    drain(u.at[pl.ds(0, CHIPS), my_half, :], s_sib.at[1])
-    drain(u.at[pl.ds(0, CHIPS - 1), my_half, :], s_ring)
+    def end(c):
+        drain(u.at[pl.ds(0, CHIPS), pl.ds(*SHARE[1 - c]), :], r_usib)
+        drain(u.at[pl.ds(0, CHIPS), pl.ds(*SHARE[c]), :], s_sib.at[1])
+        drain(u.at[pl.ds(0, CHIPS - 1), pl.ds(*SHARE[c]), :], s_ring)
+
+    pl.when(core == 0)(lambda: end(0))
+    pl.when(core == 1)(lambda: end(1))
     drain(invf.at[pl.ds(0, NY - 1)], s_y.at[0])
     drain(lg.at[pl.ds(0, NY - 1)], s_y.at[1])
 
@@ -442,7 +468,7 @@
         scratch_shapes=[
             pltpu.VMEM((CHIPS * CAP + 8, 128), f32),
             pltpu.VMEM((NB, 128), f32),
-            pltpu.VMEM((BLOCK, 128), f32),
+            pltpu.VMEM((max(SHARE[0][1], SHARE[1][1]), 128), f32),
             pltpu.VMEM((NY, NB // NY, NB), f32),
             pltpu.VMEM((NB, 128), f32),
             pltpu.VMEM((CHIPS * CAP, 128), f32),
@@ -459,51 +485,44 @@
     return hi, (v - hi.astype(f32)).astype(bf16)
 
 
-def update_kernel(tab, mat, u, sw, lg, out, l_hi, l_lo, lu):
+def update_kernel(tab, mat, u, sw, lg, out, l_cat):
     me = lax.axis_index("prow")
 
     @pl.when(pl.program_id(0) == 0)
     def _():
         hi, lo = split(lg[...])
-        l_hi[...] = hi
-        l_lo[...] = lo
-
-    uu = jnp.concatenate([u[k] for k in range(NX)], axis=1)
-    u_hi, u_lo = split(uu)
-    prod = functools.partial(jnp.dot, preferred_element_type=f32)
-    lu[...] = prod(l_hi[...], u_hi) + (prod(l_lo[...], u_hi) + prod(l_hi[...], u_lo))
-    out[...] = mat[...] - lu[...]
+        l_cat[...] = jnp.concatenate([hi, lo, hi], axis=1)
+
+    first = pl.program_id(0) * STEP
+    cols = pl.ds(pl.multiple_of(first * 128, 128), STEP * 128)
+    u_hi, u_lo = split(jnp.concatenate([u[first + k] for k in range(STEP)], axis=1))
+    out[...] = mat[:, cols] - jnp.dot(l_cat[...], jnp.concatenate([u_hi, u_hi, u_lo], axis=0), preferred_element_type=f32)
     for k in range(CAP):
         row = tab[3, k]
 
         @pl.when(row >= 0)
         def _():
-            new = jnp.concatenate([sw[t, k : k + 1, :] for t in range(NX)], axis=1)
-            out[pl.ds(row, 1), :] = new - lu[pl.ds(row, 1), :]
+            new = jnp.concatenate([sw[first + t, k : k + 1, :] for t in range(STEP)], axis=1)
+            out[pl.ds(row, 1), :] = out[pl.ds(row, 1), :] + (new - mat[pl.ds(row, 1), cols])
 
     for half in range(2):
 
         @pl.when(me == half)
         def _():
-            out[0:BLOCK, :] = jnp.concatenate([u[k, half * BLOCK : (half + 1) * BLOCK, :] for k in range(NX)], axis=1)
+            for k in range(STEP):
+                out[0:BLOCK, k * 128 : (k + 1) * 128] = u[first + k, half * BLOCK : (half + 1) * BLOCK, :]
 
 
 def update(tab, matrix, u, sw, lg):
-    width = NX * 128
+    vm = pl.BlockSpec(memory_space=pltpu.VMEM)
     return pl.pallas_call(
         update_kernel,
-        grid=(NZ,),
+        grid=(TILES // STEP,),
         out_shape=jax.ShapeDtypeStruct((ROWS, COLS), f32),
-        in_specs=[
-            pl.BlockSpec(memory_space=pltpu.SMEM),
-            pl.BlockSpec((ROWS, width), lambda g: (0, g)),
-            pl.BlockSpec((NX, NB, 128), lambda g: (g, 0, 0)),
-            pl.BlockSpec((NX, CAP, 128), lambda g: (g, 0, 0)),
-            pl.BlockSpec((ROWS, NB), lambda g: (0, 0)),
-        ],
-        out_specs=pl.BlockSpec((ROWS, width), lambda g: (0, g)),
-        scratch_shapes=[pltpu.VMEM((ROWS, NB), bf16), pltpu.VMEM((ROWS, NB), bf16), pltpu.VMEM((ROWS, width), f32)],
-        compiler_params=pltpu.CompilerParams(vmem_limit_bytes=16 << 20),
+        in_specs=[pl.BlockSpec(memory_space=pltpu.SMEM), vm, vm, vm, vm],
+        out_specs=pl.BlockSpec((ROWS, STEP * 128), lambda g: (0, g)),
+        scratch_shapes=[pltpu.VMEM((ROWS, 3 * NB), bf16)],
+        compiler_params=pltpu.CompilerParams(vmem_limit_bytes=32 << 20),
         name="update",
     )(tab, matrix, u, sw, lg)
 
@@ -540,14 +559,14 @@
 
 
 def local(matrix, lower_panel, inverse, pivots):
-    tab, comp = plan(pivots, matrix)
+    tab, comp, crowded = plan(pivots, matrix)
     u, sw, lg = move(tab, comp, matrix, lower_panel, inverse)
     lg = lg.reshape(ROWS, NB)
     result = update(tab, matrix, u, sw, lg)
     _, result = lax.while_loop(
         lambda state: state[0] > 0,
         lambda state: (jnp.int32(0), general(matrix, lg, inverse, tab[4, :NB], tab[5, :NB])),
-        (tab[6, 0], result),
+        (crowded[0, 0], result),
     )
     return result
 

time: 67.5 us -> 62.9 us (0.932)
  Pallas kernels: 64.9 us -> 60.6 us
    pallas_call x1, Pallas kernels: 53.9 us -> 51.2 us  [move(): pl.pallas_call(move_kernel, out_shape=(jax.ShapeDtypeStruct((CHIPS, NB, 1...]
    pallas_call x1, Pallas kernels: 7.94 us -> 5.74 us  [update(): pl.pallas_call(update_kernel, grid=(TILES // STEP,), out_shape=jax.ShapeD...]
where the time goes in v3:
time: 62.9 us; the launch traced here: 62.5 us
  Pallas kernels  60.6 us (96%)
  loops' own time  0.91 us (1%)
  local copies, waits for them, and re-layouts  0.73 us (1%)
    pallas_call x1, Pallas kernels, move(): pl.pallas_call(move_kernel, out_shape=(jax.ShapeDtypeStruct((CHIPS, NB, 1...  51.2 us
    pallas_call x1, Pallas kernels, update(): pl.pallas_call(update_kernel, grid=(TILES // STEP,), out_shape=jax.ShapeD...  5.74 us
    pallas_call x1, Pallas kernels, plan(): pl.pallas_call(plan_kernel, out_shape=(jax.ShapeDtypeStruct((8, 512), i32...  3.69 us

profile of v3, /device:TPU:1, one launch (start us, length us, event | category | flops | bytes accessed | tf_op | source)
XLA Modules:
  0.0 62.5 jit_solution(18265295801701237760)
XLA Ops:
  0.0 0.0 copy-start
  0.0 0.0 copy-start.1
  0.0 0.7 %copy-done.1 = s32[256]{0:T(256)S(1)} copy-done((s32[256]{0:T(256)S(1)}, s32[256]{0:T(256)}, u32[]{:S(2)}) %copy-start.1) | copy-done | bytes 1048
  0.7 0.0 copy-start.2
  0.7 3.7 %plan.1 = (s32[8,512]{1,0:T(8,128)S(1)}, f32[16,3840]{1,0:T(8,128)S(1)}, s32[1,1]{1,0:T(1,128)}) custom-call(s32[1,256]{1,0:T(1,128)S(1)} %bitcast.33, f32[384,3840]{1,0:T(8,128)} %mat.5), custom_call_target="tpu_custom_call" | custom-call | tf_op jit(solution)/shard_map/plan/pallas_call | solution.py:112
  4.4 0.0 copy-done
  4.4 51.2 %move.1 = (f32[32,256,128]{2,1,0:T(8,128)S(1)}, f32[32,16,128]{2,1,0:T(8,128)S(1)}, f32[4,96,256]{2,1,0:T(8,128)S(1)}) custom-call(s32[8,512]{1,0:T(8,128)S(1)} %get-tuple-element.77.tab, f32[16,3840]{1,0:T(8,128)S(1)} %get-tuple-element.43.comp, f32[384,3840]{1,0:T(8,128)} %mat.5, f32[96,256]{1,0:T(8,128)S(1)} %copy-done, f32[64,256]{1,0:T(8,128)} %inv.1), custom_call_target="tpu_custom_call" | custom-call | tf_op jit(solution)/shard_map/move/pallas_call | solution.py:459
  55.6 0.0 copy-start.7
  55.6 0.0 copy-done.2
  55.6 0.0 copy-start.9
  55.6 5.7 %update.1 = f32[384,3840]{1,0:T(8,128)} custom-call(s32[8,512]{1,0:T(8,128)S(1)} %get-tuple-element.77.tab, f32[384,3840]{1,0:T(8,128)S(1)} %copy-done.2, f32[32,256,128]{2,1,0:T(8,128)S(1)} %get-tuple-element.44.u, f32[32,16,128]{2,1,0:T(8,128)S(1)} %get-tuple-element.45.sw, f32[384,256]{1,0:T(8,128)S(1)} %bitcast.34), custom_call_target="tpu_custom_call" | custom-call | tf_op jit(solution)/shard_map/update/pallas_call | solution.py:518
  61.4 0.0 copy-done.7
  61.4 0.0 copy-done.9
  61.4 0.9 %while.9 = (s32[]{:T(128)}, f32[384,3840]{1,0:T(8,128)}, f32[64,256]{1,0:T(8,128)S(1)}, s32[8,512]{1,0:T(8,128)S(1)}, f32[384,3840]{1,0:T(8,128)}, /*index=5*/f32[384,256]{1,0:T(8,128)}) while((s32[]{:T(128)}, f32[384,3840]{1,0:T(8,128)}, f32[64,256]{1,0:T(8,128)S(1)}, s32[8,512]{1,0:T(8,128)S(1)}, f32[384,3840]{1,0:T(8,128)}, ...), condition=%region_2.3_spmd, body=%region_0.2_spmd | while | flops 7575514624 | bytes 526559744 | solution.py:566
Async XLA Ops:
  0.0 4.4 %copy-start = (f32[96,256]{1,0:T(8,128)S(1)}, f32[96,256]{1,0:T(8,128)}, u32[]{:S(2)}) copy-start(f32[96,256]{1,0:T(8,128)} %lp.1) | copy-start | bytes 294916
  0.0 0.7 %copy-start.1 = (s32[256]{0:T(256)S(1)}, s32[256]{0:T(256)}, u32[]{:S(2)}) copy-start(s32[256]{0:T(256)} %param.9) | copy-start | bytes 3076
  0.7 54.9 %copy-start.2 = (f32[384,3840]{1,0:T(8,128)S(1)}, f32[384,3840]{1,0:T(8,128)}, u32[]{:S(2)}) copy-start(f32[384,3840]{1,0:T(8,128)} %mat.5) | copy-start | bytes 17694724
  55.6 5.8 %copy-start.7 = (f32[4,96,256]{2,1,0:T(8,128)}, f32[4,96,256]{2,1,0:T(8,128)S(1)}, u32[]{:S(2)}) copy-start(f32[4,96,256]{2,1,0:T(8,128)S(1)} %get-tuple-element.46) | copy-start | bytes 1179652
  55.6 5.8 %copy-start.9 = (f32[64,256]{1,0:T(8,128)S(1)}, f32[64,256]{1,0:T(8,128)}, u32[]{:S(2)}) copy-start(f32[64,256]{1,0:T(8,128)} %inv.1) | copy-start | bytes 196612

commit v4 on v3

--- a/solution.py
+++ b/solution.py
@@ -130,7 +130,7 @@
 
 def move_kernel(tab, comp, mat, lp, inv, u, sw, lg, nr, top, psib, invf, orig, ret,
                 s_nr, r_nr, s_or, r_or, s_y, r_inv, r_lp, s_sib, r_psib, r_osib, s_ret, r_ret, s_ring, r_tile, r_usib,
-                relay, s_relay, r_relay):
+                relay, s_relay, r_relay, inv_cat):
     me = lax.axis_index("prow")
     yy = lax.axis_index("pcol")
     core = me % 2
@@ -226,6 +226,8 @@
 
 
     drain(invf, r_inv)
+    i_hi, i_lo = split(invf[...].reshape(NB, NB))
+    inv_cat[...] = jnp.concatenate([i_hi, i_lo, i_hi], axis=1)
 
     @pl.when(holder)
     def _():
@@ -238,8 +240,8 @@
             return 0
 
         lax.fori_loop(0, NB // 8, arrange, 0)
-        full = invf[...].reshape(NB, NB)
-        top[...] = jnp.dot(full, top[...], precision=lax.Precision.HIGHEST, preferred_element_type=f32)
+        t_hi, t_lo = split(top[...])
+        top[...] = jnp.dot(inv_cat[...], jnp.concatenate([t_hi, t_hi, t_lo], axis=0), preferred_element_type=f32)
 
         def finish(c):
             own, other = (pl.ds(*SHARE[c]), pl.ds(*SHARE[1 - c]))
@@ -390,10 +392,10 @@
             x_neighbours(back(s))
         arrived(0, x, back(4))
         onward(back(4))
-        give_back()
         for s in (1, -1):
             x_neighbours(back(s))
         x_far(z)
+        give_back()
         for s in (3, -3):
             x_neighbours(back(s))
         for s in (2, -2, 1, -1):
@@ -474,6 +476,7 @@
             pltpu.VMEM((CHIPS * CAP, 128), f32),
             dma, dma, dma, dma, dma((2,)), dma, dma, dma((3,)), dma, dma, dma, dma, dma, dma((CHIPS,)), dma,
             pltpu.VMEM((NZ, BLOCK, 128), f32), dma, dma((NZ,)),
+            pltpu.VMEM((NB, 3 * NB), bf16),
         ],
         compiler_params=pltpu.CompilerParams(collective_id=0, has_side_effects=True, vmem_limit_bytes=16 << 20),
         name="move",

time: 62.9 us -> 63 us (level)
  no operation moved by 1% of the time
where the time goes in v4:
time: 63 us; the launch traced here: 62.6 us
  Pallas kernels  60.7 us (96%)
  loops' own time  0.91 us (1%)
  local copies, waits for them, and re-layouts  0.73 us (1%)
    pallas_call x1, Pallas kernels, move(): pl.pallas_call(move_kernel, out_shape=(jax.ShapeDtypeStruct((CHIPS, NB, 1...  51.4 us
    pallas_call x1, Pallas kernels, update(): pl.pallas_call(update_kernel, grid=(TILES // STEP,), out_shape=jax.ShapeD...  5.77 us
    pallas_call x1, Pallas kernels, plan(): pl.pallas_call(plan_kernel, out_shape=(jax.ShapeDtypeStruct((8, 512), i32...  3.51 us

profile of v4, /device:TPU:1, one launch (start us, length us, event | category | flops | bytes accessed | tf_op | source)
XLA Modules:
  0.0 62.6 jit_solution(11680548487763948232)
XLA Ops:
  0.0 0.0 copy-start
  0.0 0.0 copy-start.1
  0.0 0.7 %copy-done.1 = s32[256]{0:T(256)S(1)} copy-done((s32[256]{0:T(256)S(1)}, s32[256]{0:T(256)}, u32[]{:S(2)}) %copy-start.1) | copy-done | bytes 1048
  0.7 0.0 copy-start.2
  0.7 3.5 %plan.1 = (s32[8,512]{1,0:T(8,128)S(1)}, f32[16,3840]{1,0:T(8,128)S(1)}, s32[1,1]{1,0:T(1,128)}) custom-call(s32[1,256]{1,0:T(1,128)S(1)} %bitcast.33, f32[384,3840]{1,0:T(8,128)} %mat.5), custom_call_target="tpu_custom_call" | custom-call | tf_op jit(solution)/shard_map/plan/pallas_call | solution.py:112
  4.2 0.0 copy-done
  4.2 51.4 %move.1 = (f32[32,256,128]{2,1,0:T(8,128)S(1)}, f32[32,16,128]{2,1,0:T(8,128)S(1)}, f32[4,96,256]{2,1,0:T(8,128)S(1)}) custom-call(s32[8,512]{1,0:T(8,128)S(1)} %get-tuple-element.77.tab, f32[16,3840]{1,0:T(8,128)S(1)} %get-tuple-element.43.comp, f32[384,3840]{1,0:T(8,128)} %mat.5, f32[96,256]{1,0:T(8,128)S(1)} %copy-done, f32[64,256]{1,0:T(8,128)} %inv.1), custom_call_target="tpu_custom_call" | custom-call | tf_op jit(solution)/shard_map/move/pallas_call | solution.py:461
  55.7 0.0 copy-start.7
  55.7 0.0 copy-done.2
  55.7 0.0 copy-start.9
  55.7 5.8 %update.1 = f32[384,3840]{1,0:T(8,128)} custom-call(s32[8,512]{1,0:T(8,128)S(1)} %get-tuple-element.77.tab, f32[384,3840]{1,0:T(8,128)S(1)} %copy-done.2, f32[32,256,128]{2,1,0:T(8,128)S(1)} %get-tuple-element.44.u, f32[32,16,128]{2,1,0:T(8,128)S(1)} %get-tuple-element.45.sw, f32[384,256]{1,0:T(8,128)S(1)} %bitcast.34), custom_call_target="tpu_custom_call" | custom-call | tf_op jit(solution)/shard_map/update/pallas_call | solution.py:521
  61.5 0.0 copy-done.7
  61.5 0.0 copy-done.9
  61.5 0.9 %while.9 = (s32[]{:T(128)}, f32[384,3840]{1,0:T(8,128)}, f32[64,256]{1,0:T(8,128)S(1)}, s32[8,512]{1,0:T(8,128)S(1)}, f32[384,3840]{1,0:T(8,128)}, /*index=5*/f32[384,256]{1,0:T(8,128)}) while((s32[]{:T(128)}, f32[384,3840]{1,0:T(8,128)}, f32[64,256]{1,0:T(8,128)S(1)}, s32[8,512]{1,0:T(8,128)S(1)}, f32[384,3840]{1,0:T(8,128)}, ...), condition=%region_2.3_spmd, body=%region_0.2_spmd | while | flops 7575514624 | bytes 526559744 | solution.py:569
Async XLA Ops:
  0.0 4.2 %copy-start = (f32[96,256]{1,0:T(8,128)S(1)}, f32[96,256]{1,0:T(8,128)}, u32[]{:S(2)}) copy-start(f32[96,256]{1,0:T(8,128)} %lp.1) | copy-start | bytes 294916
  0.0 0.7 %copy-start.1 = (s32[256]{0:T(256)S(1)}, s32[256]{0:T(256)}, u32[]{:S(2)}) copy-start(s32[256]{0:T(256)} %param.9) | copy-start | bytes 3076
  0.7 55.0 %copy-start.2 = (f32[384,3840]{1,0:T(8,128)S(1)}, f32[384,3840]{1,0:T(8,128)}, u32[]{:S(2)}) copy-start(f32[384,3840]{1,0:T(8,128)} %mat.5) | copy-start | bytes 17694724
  55.7 5.8 %copy-start.7 = (f32[4,96,256]{2,1,0:T(8,128)}, f32[4,96,256]{2,1,0:T(8,128)S(1)}, u32[]{:S(2)}) copy-start(f32[4,96,256]{2,1,0:T(8,128)S(1)} %get-tuple-element.46) | copy-start | bytes 1179652
  55.7 5.8 %copy-start.9 = (f32[64,256]{1,0:T(8,128)S(1)}, f32[64,256]{1,0:T(8,128)}, u32[]{:S(2)}) copy-start(f32[64,256]{1,0:T(8,128)} %inv.1) | copy-start | bytes 196612

commit v5 on v4

--- a/solution.py
+++ b/solution.py
@@ -13,7 +13,7 @@
 NX, NZ, NY = 4, 8, 4
 N_PROW = 64
 CHIPS = NX * NZ
-STEP = 10
+STEP = 15
 SHARE = ((0, 112), (112, 144))
 AWAY = (4, 3, 5, 2, 6, 1, 7)
 TILES = 30

time: 63 us -> 62.6 us (level)
  no operation moved by 1% of the time
where the time goes in v5:
time: 62.6 us; the launch traced here: 62.5 us
  Pallas kernels  60.6 us (97%)
  loops' own time  0.91 us (1%)
  local copies, waits for them, and re-layouts  0.73 us (1%)
    pallas_call x1, Pallas kernels, move(): pl.pallas_call(move_kernel, out_shape=(jax.ShapeDtypeStruct((CHIPS, NB, 1...  51.1 us
    pallas_call x1, Pallas kernels, update(): pl.pallas_call(update_kernel, grid=(TILES // STEP,), out_shape=jax.ShapeD...  5.75 us
    pallas_call x1, Pallas kernels, plan(): pl.pallas_call(plan_kernel, out_shape=(jax.ShapeDtypeStruct((8, 512), i32...  3.76 us

profile of v5, /device:TPU:1, one launch (start us, length us, event | category | flops | bytes accessed | tf_op | source)
XLA Modules:
  0.0 62.5 jit_solution(1486928113240789844)
XLA Ops:
  0.0 0.0 copy-start
  0.0 0.0 copy-start.1
  0.0 0.7 %copy-done.1 = s32[256]{0:T(256)S(1)} copy-done((s32[256]{0:T(256)S(1)}, s32[256]{0:T(256)}, u32[]{:S(2)}) %copy-start.1) | copy-done | bytes 1048
  0.7 0.0 copy-start.2
  0.7 3.8 %plan.1 = (s32[8,512]{1,0:T(8,128)S(1)}, f32[16,3840]{1,0:T(8,128)S(1)}, s32[1,1]{1,0:T(1,128)}) custom-call(s32[1,256]{1,0:T(1,128)S(1)} %bitcast.33, f32[384,3840]{1,0:T(8,128)} %mat.5), custom_call_target="tpu_custom_call" | custom-call | tf_op jit(solution)/shard_map/plan/pallas_call | solution.py:112
  4.5 0.0 copy-done
  4.5 51.1 %move.1 = (f32[32,256,128]{2,1,0:T(8,128)S(1)}, f32[32,16,128]{2,1,0:T(8,128)S(1)}, f32[4,96,256]{2,1,0:T(8,128)S(1)}) custom-call(s32[8,512]{1,0:T(8,128)S(1)} %get-tuple-element.77.tab, f32[16,3840]{1,0:T(8,128)S(1)} %get-tuple-element.43.comp, f32[384,3840]{1,0:T(8,128)} %mat.5, f32[96,256]{1,0:T(8,128)S(1)} %copy-done, f32[64,256]{1,0:T(8,128)} %inv.1), custom_call_target="tpu_custom_call" | custom-call | tf_op jit(solution)/shard_map/move/pallas_call | solution.py:461
  55.6 0.0 copy-start.7
  55.6 0.0 copy-done.2
  55.7 0.0 copy-start.9
  55.7 5.8 %update.1 = f32[384,3840]{1,0:T(8,128)} custom-call(s32[8,512]{1,0:T(8,128)S(1)} %get-tuple-element.77.tab, f32[384,3840]{1,0:T(8,128)S(1)} %copy-done.2, f32[32,256,128]{2,1,0:T(8,128)S(1)} %get-tuple-element.44.u, f32[32,16,128]{2,1,0:T(8,128)S(1)} %get-tuple-element.45.sw, f32[384,256]{1,0:T(8,128)S(1)} %bitcast.34), custom_call_target="tpu_custom_call" | custom-call | tf_op jit(solution)/shard_map/update/pallas_call | solution.py:521
  61.4 0.0 copy-done.7
  61.4 0.0 copy-done.9
  61.4 0.9 %while.9 = (s32[]{:T(128)}, f32[384,3840]{1,0:T(8,128)}, f32[64,256]{1,0:T(8,128)S(1)}, s32[8,512]{1,0:T(8,128)S(1)}, f32[384,3840]{1,0:T(8,128)}, /*index=5*/f32[384,256]{1,0:T(8,128)}) while((s32[]{:T(128)}, f32[384,3840]{1,0:T(8,128)}, f32[64,256]{1,0:T(8,128)S(1)}, s32[8,512]{1,0:T(8,128)S(1)}, f32[384,3840]{1,0:T(8,128)}, ...), condition=%region_2.3_spmd, body=%region_0.2_spmd | while | flops 7575514624 | bytes 526559744 | solution.py:569
Async XLA Ops:
  0.0 4.5 %copy-start = (f32[96,256]{1,0:T(8,128)S(1)}, f32[96,256]{1,0:T(8,128)}, u32[]{:S(2)}) copy-start(f32[96,256]{1,0:T(8,128)} %lp.1) | copy-start | bytes 294916
  0.0 0.7 %copy-start.1 = (s32[256]{0:T(256)S(1)}, s32[256]{0:T(256)}, u32[]{:S(2)}) copy-start(s32[256]{0:T(256)} %param.9) | copy-start | bytes 3076
  0.7 54.9 %copy-start.2 = (f32[384,3840]{1,0:T(8,128)S(1)}, f32[384,3840]{1,0:T(8,128)}, u32[]{:S(2)}) copy-start(f32[384,3840]{1,0:T(8,128)} %mat.5) | copy-start | bytes 17694724
  55.6 5.8 %copy-start.7 = (f32[4,96,256]{2,1,0:T(8,128)}, f32[4,96,256]{2,1,0:T(8,128)S(1)}, u32[]{:S(2)}) copy-start(f32[4,96,256]{2,1,0:T(8,128)S(1)} %get-tuple-element.46) | copy-start | bytes 1179652
  55.7 5.8 %copy-start.9 = (f32[64,256]{1,0:T(8,128)S(1)}, f32[64,256]{1,0:T(8,128)}, u32[]{:S(2)}) copy-start(f32[64,256]{1,0:T(8,128)} %inv.1) | copy-start | bytes 196612
